TPU v7x, 512 devices: a whole 4x8x8 slice. The times are simulated.
512 devices in a mesh: dp: 64 (over y, z), tower: 8 (over x, core).
Axes of the slice: x: 4, y: 8, z: 8, core: 2. Of those that a mesh axis runs over, the one named last changes fastest.
Arguments:
- rep: bfloat16 [16384, 2048], P('dp', 'tower'), may hold values from -6 to 6
- arm_ids: int32 [16384], P('dp'), may hold values from 0 to 63, as said below
- outcome: bfloat16 [16384], P('dp'), may hold values from -6 to 6
- weight: bfloat16 [16384], P('dp'), may hold values from 0.5 to 4
- w_hidden: bfloat16 [64, 2048, 2048], P('dp', None, 'tower'), may hold values from -0.125 to 0.125
- b_hidden: float32 [64, 2048], P('dp', 'tower'), may hold values from -3 to 3
- w_head: float32 [64, 2048], P('dp', 'tower'), may hold values from -0.125 to 0.125
- b_head: float32 [64], P('dp'), may hold values from -4 to 4
Outputs:
- grad_hidden: float32 [64, 2048, 2048], P('dp', None, 'tower')
- grad_hidden_bias: float32 [64, 2048], P('dp', 'tower')
- grad_head: float32 [64, 2048], P('dp', 'tower')
- grad_head_bias: float32 [64], P('dp')
- grad_rep: bfloat16 [16384, 2048], P('dp', 'tower')
- predicted: bfloat16 [16384], P('dp')
Inputs may be any that keep to these rules, and one draw needn't show every extreme that they name: `arm_ids`: among the 256 rows of one index of dp at most 14 name one arm, and in every draw some index has an arm named exactly 14 times; over all 16384 rows at most 512 name one arm, and in every draw some arm is named exactly 512 times.
All inputs are finite; a program needn't handle non-finite values.
Results may differ from a plain program's by a relative error of at most 0.019.
Values may be sent and summed in bfloat16 or wider, within the bound.
No kernel may reach another device: no remote copies, remote signals or barrier semaphores. Data moves between devices by JAX's collectives and lax.ppermute only.
A program may use at most 64 MiB of HBM per device.

v0:
```python
import jax
import jax.numpy as jnp
from jax import lax
from jax.sharding import PartitionSpec as P


def arm_slots(arm_ids, arm_count, slot_depth):
    arm_labels = jnp.arange(arm_count, dtype=jnp.int32)
    one_hot = (arm_ids[:, None] == arm_labels[None, :]).astype(jnp.int32)
    arm_rank = jnp.sum(jnp.cumsum(one_hot, axis=0) * one_hot, axis=1) - 1
    return arm_ids * slot_depth + arm_rank


def fill_slots(values, slot_index, slot_total):
    row_count = values.shape[0]
    source_row = (
        jnp.full((slot_total,), row_count, jnp.int32)
        .at[slot_index]
        .set(jnp.arange(row_count, dtype=jnp.int32))
    )
    padded_rows = jnp.concatenate(
        [values, jnp.zeros((1,) + values.shape[1:], values.dtype)], axis=0
    )
    return padded_rows[source_row]


def tower_step(inputs, targets, weights, matrix, bias_cols, head_cols, head_bias):
    pre_act = jnp.dot(inputs, matrix, preferred_element_type=jnp.float32) + bias_cols
    sigmoid_pre = jax.nn.sigmoid(pre_act)
    activation = pre_act * sigmoid_pre
    pred_share = jnp.sum(activation * head_cols, axis=1)
    full_pred = lax.psum(pred_share, "tower") + head_bias
    resid_grad = weights * (full_pred - targets)
    pre_grad = resid_grad[:, None] * head_cols * sigmoid_pre * (1.0 + pre_act * (1.0 - sigmoid_pre))
    pre_grad_half = pre_grad.astype(jnp.bfloat16)
    grad_matrix = lax.dot_general(
        inputs, pre_grad_half, (((0,), (0,)), ((), ())), preferred_element_type=jnp.float32
    )
    grad_bias = jnp.sum(pre_grad, axis=0)
    grad_vector = jnp.sum(resid_grad[:, None] * activation, axis=0)
    grad_scalar = jnp.sum(resid_grad)
    return (full_pred, pre_grad_half, grad_matrix, grad_bias, grad_vector, grad_scalar)


def body(rep, arm_ids, outcome, weight, w_hidden, b_hidden, w_head, b_head):
    arm_count = lax.axis_size("dp")
    row_count = arm_ids.shape[0]
    slot_depth = 7 * (row_count // (2 * arm_count))
    slot_total = arm_count * slot_depth
    slot_index = arm_slots(arm_ids, arm_count, slot_depth)
    side_data = fill_slots(jnp.stack([outcome, weight], axis=1), slot_index, slot_total).reshape(
        arm_count, slot_depth, 2
    )
    matrix = w_hidden[0]
    bias_cols = b_hidden[0]
    head_cols = w_head[0]
    head_bias = b_head[0]
    wide_rep = lax.all_gather(rep, "tower", axis=1, tiled=True)
    wide_slots = fill_slots(wide_rep, slot_index, slot_total).reshape(
        arm_count, slot_depth, wide_rep.shape[1]
    )
    arrived, arrived_side = (
        lax.all_to_all(wide_slots, "dp", split_axis=0, concat_axis=0, tiled=True),
        lax.all_to_all(side_data, "dp", split_axis=0, concat_axis=0, tiled=True),
    )
    slot_rows = arrived.reshape(slot_total, arrived.shape[2])
    arrived_side = arrived_side.reshape(slot_total, 2).astype(jnp.float32)
    targets = arrived_side[:, 0]
    weights = arrived_side[:, 1]
    full_pred, pre_grad_half, grad_matrix, grad_bias, grad_vector, grad_scalar = tower_step(
        slot_rows, targets, weights, matrix, bias_cols, head_cols, head_bias
    )
    pred_half = full_pred.astype(jnp.bfloat16)
    partial_full = lax.dot_general(
        pre_grad_half, matrix, (((1,), (1,)), ((), ())), preferred_element_type=jnp.float32
    ).astype(jnp.bfloat16)
    full_width = partial_full.shape[1]
    returned, pred_back = (
        lax.all_to_all(
            partial_full.reshape(arm_count, slot_depth, full_width),
            "dp",
            split_axis=0,
            concat_axis=0,
            tiled=True,
        ),
        lax.all_to_all(
            pred_half.reshape(arm_count, slot_depth), "dp", split_axis=0, concat_axis=0, tiled=True
        ),
    )
    row_partial = returned.reshape(slot_total, full_width)[slot_index]
    grad_rep = lax.psum_scatter(
        row_partial.astype(jnp.float32).astype(jnp.bfloat16),
        "tower",
        scatter_dimension=1,
        tiled=True,
    )
    predicted = pred_back.reshape(slot_total)[slot_index]
    return (
        grad_matrix[None],
        grad_bias[None],
        grad_vector[None],
        grad_scalar.reshape(1),
        grad_rep,
        predicted,
    )


def solution(mesh):
    return jax.shard_map(
        body,
        mesh=mesh,
        in_specs=(
            P("dp", "tower"),
            P("dp"),
            P("dp"),
            P("dp"),
            P("dp", None, "tower"),
            P("dp", "tower"),
            P("dp", "tower"),
            P("dp"),
        ),
        out_specs=(
            P("dp", None, "tower"),
            P("dp", "tower"),
            P("dp", "tower"),
            P("dp"),
            P("dp", "tower"),
            P("dp"),
        ),
        check_vma=False,
    )
```

profile of v0, /device:TPU:8, one launch (start us, length us, event | category | flops | bytes accessed | tf_op | source)
XLA Modules:
  0.0 430.2 jit_solution(11687043676716487167)
XLA Ops:
  7.2 0.0 copy-start
  7.2 0.0 all-gather.2.cloned.1.call-start
  7.2 0.7 all-gather.2.cloned.1.call-update
  7.9 0.7 fusion.7
  8.6 0.6 reduce-window.6
  9.2 0.2 slice_reduce_fusion
  9.4 0.7 stack.10
  10.1 0.7 stack.9
  10.8 0.1 copy.25
  11.0 0.8 fusion.6
  11.7 0.7 compare_select_fusion.1
  12.4 1.4 scatter_custom_fusion
  13.9 2.4 gather_fusion.1
  16.3 0.1 copy.26
  16.4 0.2 reshape.61
  16.6 0.7 copy.27
  17.2 16.6 %all-to-all-start.1 = ((bf16[64,14,2]{1,2,0:T(2,128)(2,1)}), bf16[64,14,2]{1,2,0:T(2,128)(2,1)S(1)}, u32[]{:S(2)}, u32[]{:S(2)}) async-start(bf16[64,14,2]{1,2,0:T(2,128)(2,1)} %copy.27), calls=%async_computation.1 | async-start | bytes 65536 | tf_op jit(solution)/shard_map/all_to_all | solution.py:64
  33.8 9.6 %all-gather.2.cloned.1.call-done = bf16[256,2048]{1,0:T(8,128)(2,1)} async-done(((bf16[256,256]{1,0:T(8,128)(2,1)}), bf16[256,2048]{1,0:T(8,128)(2,1)}) %all-gather.2.cloned.1.call-update) | async-done | bytes 1048592 | tf_op jit(solution)/shard_map/all_gather | solution.py:58
  43.4 1.3 concatenate.6
  44.7 5.0 %gather_fusion = bf16[896,2048]{1,0:T(8,128)(2,1)} fusion(bf16[257,2048]{1,0:T(8,128)(2,1)S(1)} %concatenate.6, s32[1024]{0:T(1024)S(1)} %pad_clamp_fusion.1), kind=kCustom, calls=%fused_computation | custom fusion | bytes 7343616 | tf_op jit(solution)/shard_map/gather | solution.py:24
  49.8 6.0 %reshape.59 = bf16[64,14,2048]{2,1,0:T(8,128)(2,1)} reshape(bf16[896,2048]{1,0:T(8,128)(2,1)} %gather_fusion) | data formatting | bytes 7340032 | tf_op jit(solution)/shard_map/reshape | solution.py:59
  55.8 0.0 all-to-all-done.1
  55.8 13.6 %all-to-all-start = ((bf16[64,14,2048]{2,1,0:T(8,128)(2,1)}), bf16[64,14,2048]{2,1,0:T(8,128)(2,1)}, u32[]{:S(2)}, u32[]{:S(2)}) async-start(bf16[64,14,2048]{2,1,0:T(8,128)(2,1)} %reshape.59), calls=%async_computation | async-start | bytes 8388608 | tf_op jit(solution)/shard_map/all_to_all | solution.py:63
  70.0 0.1 copy.28
  70.1 0.1 copy.29
  70.2 0.1 reshape.66
  70.4 0.0 copy-start.1
  70.4 0.0 copy-start.2
  70.4 127.5 %all-to-all-done = bf16[64,14,2048]{2,1,0:T(8,128)(2,1)} async-done(((bf16[64,14,2048]{2,1,0:T(8,128)(2,1)}), bf16[64,14,2048]{2,1,0:T(8,128)(2,1)}, u32[]{:S(2)}, u32[]{:S(2)}) %all-to-all-start) | async-done | bytes 3670048 | tf_op jit(solution)/shard_map/all_to_all | solution.py:63
  197.9 5.8 %reshape.60 = bf16[896,2048]{1,0:T(8,128)(2,1)} reshape(bf16[64,14,2048]{2,1,0:T(8,128)(2,1)} %all-to-all-done) | data formatting | bytes 7340032 | tf_op jit(solution)/shard_map/reshape | solution.py:66
  203.8 0.0 copy-done
  203.8 0.0 copy-done.1
  203.8 0.0 copy-done.2
  203.8 3.3 multiply_reduce_fusion.1
  207.1 12.4 %psum.7 = f32[896]{0:T(1024)S(1)} all-reduce(f32[896]{0:T(1024)S(1)} %get-tuple-element.13), channel_id=1, replica_groups=mesh['dp'=64,'tower'=8] {'tower'}, use_global_device_ids=true, to_apply=%region_5.6 | all-reduce | flops 896 | bytes 7168 | tf_op jit(solution)/shard_map/psum | solution.py:32
  219.5 0.6 fusion.11
  220.1 3.1 convolution_convert_fusion
  223.2 6.0 %reshape.63 = bf16[64,14,2048]{2,1,0:T(8,128)(2,1)} reshape(bf16[896,2048]{1,0:T(8,128)(2,1)} %convolution_convert_fusion) | data formatting | bytes 7340032 | tf_op jit(solution)/shard_map/reshape | solution.py:80
  229.2 16.0 %all-to-all-start.2 = ((bf16[64,14,2048]{2,1,0:T(8,128)(2,1)}), bf16[64,14,2048]{2,1,0:T(8,128)(2,1)}, u32[]{:S(2)}, u32[]{:S(2)}) async-start(bf16[64,14,2048]{2,1,0:T(8,128)(2,1)} %reshape.63), calls=%async_computation.2 | async-start | bytes 8388608 | tf_op jit(solution)/shard_map/all_to_all | solution.py:79
  245.2 0.2 reduce-scatter.2.cloned.1.call-start
  245.4 123.7 %all-to-all-done.2 = bf16[64,14,2048]{2,1,0:T(8,128)(2,1)} async-done(((bf16[64,14,2048]{2,1,0:T(8,128)(2,1)}), bf16[64,14,2048]{2,1,0:T(8,128)(2,1)}, u32[]{:S(2)}, u32[]{:S(2)}) %all-to-all-start.2) | async-done | bytes 3670048 | tf_op jit(solution)/shard_map/all_to_all | solution.py:79
  369.1 6.0 %reshape.64 = bf16[896,2048]{1,0:T(8,128)(2,1)} reshape(bf16[64,14,2048]{2,1,0:T(8,128)(2,1)} %all-to-all-done.2) | data formatting | bytes 7340032 | tf_op jit(solution)/shard_map/reshape | solution.py:90
  375.1 5.9 %gather_fusion.2 = bf16[256,2048]{1,0:T(8,128)(2,1)} fusion(bf16[896,2048]{1,0:T(8,128)(2,1)} %reshape.64, s32[1024]{0:T(1024)S(1)} %pad_clamp_fusion), kind=kCustom, calls=%fused_computation.2 | custom fusion | bytes 2098176 | tf_op jit(solution)/shard_map/gather | solution.py:90
  380.9 0.0 reduce-scatter.2.cloned.1.call-update
  380.9 0.8 all_to_all.20
  381.7 13.4 %all-to-all-start.3 = ((bf16[64,1,14]{2,1,0:T(2,128)(2,1)}), bf16[64,1,14]{2,1,0:T(2,128)(2,1)S(1)}, u32[]{:S(2)}, u32[]{:S(2)}) async-start(bf16[64,1,14]{2,1,0:T(2,128)(2,1)} %all_to_all.20), calls=%async_computation.4 | async-start | bytes 65536 | tf_op jit(solution)/shard_map/all_to_all | solution.py:86
  395.1 4.9 %convolution_bitcast_fusion = f32[1,2048,256]{2,1,0:T(8,128)} fusion(bf16[896,2048]{1,0:T(8,128)(2,1)} %reshape.60, f32[896,256]{1,0:T(8,128)S(1)} %get-tuple-element.14, f32[896]{0:T(1024)S(1)} %get-tuple-element.11, f32[256]{0:T(256)S(1)} %bitcast.41), kind=kOutput, calls=%fused_computation.6 | convolution fusion | flops 941817856 | bytes 6689280 | tf_op jit(solution)/shard_map/dot_general | solution.py:36
  400.0 1.1 multiply_reduce_fusion
  401.1 5.0 %all-to-all-done.3 = bf16[64,1,14]{2,1,0:T(2,128)(2,1)S(1)} async-done(((bf16[64,1,14]{2,1,0:T(2,128)(2,1)}), bf16[64,1,14]{2,1,0:T(2,128)(2,1)S(1)}, u32[]{:S(2)}, u32[]{:S(2)}) %all-to-all-start.3) | async-done | bytes 1824 | tf_op jit(solution)/shard_map/all_to_all | solution.py:86
  406.1 0.1 reduce.3
  406.2 0.1 reshape.65
  406.3 2.4 gather_fusion.3
  408.8 14.5 %reduce-scatter.2.cloned.1.call-done = bf16[256,256]{1,0:T(8,128)(2,1)} async-done(((bf16[256,2048]{1,0:T(8,128)(2,1)}), bf16[256,256]{1,0:T(8,128)(2,1)}) %reduce-scatter.2.cloned.1.call-update) | async-done | bytes 131088 | tf_op jit(solution)/shard_map/reduce_scatter | solution.py:91
  (9 shorter events, 0.1 us)
Async XLA Ops:
  7.2 196.6 %copy-start = (bf16[1,2048,256]{2,1,0:T(8,128)(2,1)S(1)}, bf16[1,2048,256]{2,1,0:T(8,128)(2,1)}, u32[]{:S(2)}) copy-start(bf16[1,2048,256]{2,1,0:T(8,128)(2,1)} %param.12) | copy-start | bytes 3145732
  7.2 36.3 %all-gather.2.cloned.1.call-start = ((), (), s32[]{:S(2)}) async-start(), calls=%async_computation.5 | async-start | bytes 1179648 | tf_op jit(solution)/shard_map/all_gather | solution.py:58
  17.2 38.5 %all-to-all-start.1 = ((bf16[64,14,2]{1,2,0:T(2,128)(2,1)}), bf16[64,14,2]{1,2,0:T(2,128)(2,1)S(1)}, u32[]{:S(2)}, u32[]{:S(2)}) async-start(bf16[64,14,2]{1,2,0:T(2,128)(2,1)} %copy.27), calls=%async_computation.1 | async-start | bytes 65536 | tf_op jit(solution)/shard_map/all_to_all | solution.py:64
  55.8 142.2 %all-to-all-start = ((bf16[64,14,2048]{2,1,0:T(8,128)(2,1)}), bf16[64,14,2048]{2,1,0:T(8,128)(2,1)}, u32[]{:S(2)}, u32[]{:S(2)}) async-start(bf16[64,14,2048]{2,1,0:T(8,128)(2,1)} %reshape.59), calls=%async_computation | async-start | bytes 8388608 | tf_op jit(solution)/shard_map/all_to_all | solution.py:63
  70.4 133.4 %copy-start.1 = (f32[1,256]{1,0:T(1,128)S(1)}, f32[1,256]{1,0:T(1,128)}, u32[]{:S(2)}) copy-start(f32[1,256]{1,0:T(1,128)} %param.14) | copy-start | bytes 3076
  70.4 133.4 %copy-start.2 = (f32[1,256]{1,0:T(1,128)S(1)}, f32[1,256]{1,0:T(1,128)}, u32[]{:S(2)}) copy-start(f32[1,256]{1,0:T(1,128)} %param.13) | copy-start | bytes 3076
  229.2 139.9 %all-to-all-start.2 = ((bf16[64,14,2048]{2,1,0:T(8,128)(2,1)}), bf16[64,14,2048]{2,1,0:T(8,128)(2,1)}, u32[]{:S(2)}, u32[]{:S(2)}) async-start(bf16[64,14,2048]{2,1,0:T(8,128)(2,1)} %reshape.63), calls=%async_computation.2 | async-start | bytes 8388608 | tf_op jit(solution)/shard_map/all_to_all | solution.py:79
  245.2 178.2 %reduce-scatter.2.cloned.1.call-start = ((), (), s32[]{:S(2)}) async-start(), calls=%async_computation.6 | async-start | bytes 1179648 | tf_op jit(solution)/shard_map/reduce_scatter | solution.py:91
  381.7 24.4 %all-to-all-start.3 = ((bf16[64,1,14]{2,1,0:T(2,128)(2,1)}), bf16[64,1,14]{2,1,0:T(2,128)(2,1)S(1)}, u32[]{:S(2)}, u32[]{:S(2)}) async-start(bf16[64,1,14]{2,1,0:T(2,128)(2,1)} %all_to_all.20), calls=%async_computation.4 | async-start | bytes 65536 | tf_op jit(solution)/shard_map/all_to_all | solution.py:86
Sparse Core Ops, SparseCore 0:
  10.1 33.2 all-gather.1
  381.1 42.2 reduce-scatter.1
where the time goes:
time: 431 us; the launch traced here: 430 us
  waiting for transfers between devices  281 us (65%)
  starting transfers between devices  59.7 us (14%)
  local copies, waits for them, and re-layouts  46.2 us (11%)
  between operations  14.8 us (3%)
  blocking collectives  12.4 us (3%)
  matrix products  11.3 us (3%)
  other arithmetic  4.59 us (1%)
    all_to_all x1, waiting for transfers between devices, body(): lax.all_to_all(wide_slots, 'dp', split_axis=0, concat_axis=0, tiled=True)  128 us
    all_to_all x1, waiting for transfers between devices, body(): lax.all_to_all(partial_full.reshape(arm_count, slot_depth, full_width), '...  124 us
    all_to_all x1, starting transfers between devices, body(): lax.all_to_all(side_data, 'dp', split_axis=0, concat_axis=0, tiled=True)  16.6 us
    all_to_all x1, starting transfers between devices, body(): lax.all_to_all(partial_full.reshape(arm_count, slot_depth, full_width), '...  16 us
    reduce_scatter x1, waiting for transfers between devices, body(): lax.psum_scatter(row_partial.astype(jnp.float32).astype(jnp.bfloat16), 't...  14.5 us
    all_to_all x1, starting transfers between devices, body(): lax.all_to_all(wide_slots, 'dp', split_axis=0, concat_axis=0, tiled=True)  13.6 us
    all_to_all x1, starting transfers between devices, body(): lax.all_to_all(pred_half.reshape(arm_count, slot_depth), 'dp', split_axis...  13.4 us
    psum x1, blocking collectives, tower_step(): full_pred = lax.psum(pred_share, 'tower') + head_bias  12.4 us
  transfers between devices with their start and end apart: 6, of which 5 were waited for; matrix products, arithmetic and copies ran while one was open for 7% of the time, Pallas kernels for 0%

commit v1 on v0

--- a/solution.py
+++ b/solution.py
@@ -55,7 +55,9 @@
     bias_cols = b_hidden[0]
     head_cols = w_head[0]
     head_bias = b_head[0]
-    wide_rep = lax.all_gather(rep, "tower", axis=1, tiled=True)
+    wide_rep = jnp.concatenate(
+        lax.all_to_all(jnp.stack([rep] * lax.axis_size("tower")), "tower", 0, 0), axis=1
+    )
     wide_slots = fill_slots(wide_rep, slot_index, slot_total).reshape(
         arm_count, slot_depth, wide_rep.shape[1]
     )

time: 431 us -> 435 us (level)
  starting transfers between devices: 59.7 us -> 64.8 us
    all_gather x1 -> x0, waiting for transfers between devices: 9.63 us -> none  [body(): wide_rep = lax.all_gather(rep, 'tower', axis=1, tiled=True)]
    all_to_all x0 -> x1, waiting for transfers between devices: none -> 8 us  [body(): lax.all_to_all(jnp.stack([rep] * lax.axis_size('tower')), 'tower', 0, 0)]
where the time goes in v1:
time: 435 us; the launch traced here: 434 us
  waiting for transfers between devices  280 us (64%)
  starting transfers between devices  64.8 us (15%)
  local copies, waits for them, and re-layouts  47.1 us (11%)
  between operations  14.9 us (3%)
  blocking collectives  12.4 us (3%)
  matrix products  11.4 us (3%)
    all_to_all x1, waiting for transfers between devices, body(): lax.all_to_all(wide_slots, 'dp', split_axis=0, concat_axis=0, tiled=True)  130 us
    all_to_all x1, waiting for transfers between devices, body(): lax.all_to_all(partial_full.reshape(arm_count, slot_depth, full_width), '...  120 us
    all_to_all x1, starting transfers between devices, body(): lax.all_to_all(pred_half.reshape(arm_count, slot_depth), 'dp', split_axis...  17.6 us
    reduce_scatter x1, waiting for transfers between devices, body(): lax.psum_scatter(row_partial.astype(jnp.float32).astype(jnp.bfloat16), 't...  16.7 us
    all_to_all x1, starting transfers between devices, body(): lax.all_to_all(side_data, 'dp', split_axis=0, concat_axis=0, tiled=True)  16.6 us
    all_to_all x1, starting transfers between devices, body(): lax.all_to_all(partial_full.reshape(arm_count, slot_depth, full_width), '...  13.2 us
    all_to_all x1, starting transfers between devices, body(): lax.all_to_all(wide_slots, 'dp', split_axis=0, concat_axis=0, tiled=True)  12.9 us
    psum x1, blocking collectives, tower_step(): full_pred = lax.psum(pred_share, 'tower') + head_bias  12.4 us
  transfers between devices with their start and end apart: 6, of which 5 were waited for; matrix products, arithmetic and copies ran while one was open for 7% of the time, Pallas kernels for 0%

profile of v1, /device:TPU:8, one launch (start us, length us, event | category | flops | bytes accessed | tf_op | source)
XLA Modules:
  0.0 433.6 jit_solution(12433955735760482851)
XLA Ops:
  7.2 0.0 copy-start
  7.2 0.0 copy-start.1
  7.2 2.0 stack.8
  9.2 4.3 all-to-all-start
  13.5 0.7 fusion.7
  14.2 0.6 reduce-window.6
  14.8 0.2 slice_reduce_fusion
  15.0 0.7 stack.10
  15.7 0.7 stack.9
  16.4 0.1 copy.27
  16.6 0.0 copy-done.1
  16.6 0.1 fusion.6
  16.7 1.4 scatter_custom_fusion
  18.1 2.4 gather_fusion.1
  20.5 0.1 copy.28
  20.7 0.2 reshape.71
  20.8 0.7 copy.29
  21.5 8.0 %all-to-all-done = bf16[8,256,256]{2,1,0:T(8,128)(2,1)S(1)} async-done(((bf16[8,256,256]{2,1,0:T(8,128)(2,1)}), bf16[8,256,256]{2,1,0:T(8,128)(2,1)S(1)}, u32[]{:S(2)}, u32[]{:S(2)}) %all-to-all-start) | async-done | bytes 1048608 | tf_op jit(solution)/shard_map/all_to_all | solution.py:59
  29.5 16.6 %all-to-all-start.2 = ((bf16[64,14,2]{1,2,0:T(2,128)(2,1)}), bf16[64,14,2]{1,2,0:T(2,128)(2,1)S(1)}, u32[]{:S(2)}, u32[]{:S(2)}) async-start(bf16[64,14,2]{1,2,0:T(2,128)(2,1)} %copy.29), calls=%async_computation.2 | async-start | bytes 65536 | tf_op jit(solution)/shard_map/all_to_all | solution.py:66
  46.1 0.1 copy.33
  46.2 0.1 concatenate.6
  46.3 5.0 %gather_fusion = bf16[896,2048]{1,0:T(8,128)(2,1)} fusion(bf16[257,2048]{1,0:T(8,128)(2,1)S(1)} %concatenate.6, s32[1024]{0:T(1024)S(1)} %pad_clamp_fusion.1), kind=kCustom, calls=%fused_computation | custom fusion | bytes 7343616 | tf_op jit(solution)/shard_map/gather | solution.py:24
  51.3 6.0 %reshape.69 = bf16[64,14,2048]{2,1,0:T(8,128)(2,1)} reshape(bf16[896,2048]{1,0:T(8,128)(2,1)} %gather_fusion) | data formatting | bytes 7340032 | tf_op jit(solution)/shard_map/reshape | solution.py:61
  57.3 0.0 all-to-all-done.2
  57.3 12.9 %all-to-all-start.1 = ((bf16[64,14,2048]{2,1,0:T(8,128)(2,1)}), bf16[64,14,2048]{2,1,0:T(8,128)(2,1)}, u32[]{:S(2)}, u32[]{:S(2)}) async-start(bf16[64,14,2048]{2,1,0:T(8,128)(2,1)} %reshape.69), calls=%async_computation.1 | async-start | bytes 8388608 | tf_op jit(solution)/shard_map/all_to_all | solution.py:65
  70.9 0.1 copy.30
  71.0 0.1 copy.31
  71.1 0.1 reshape.76
  71.3 0.0 copy-start.2
  71.3 0.0 copy-start.3
  71.3 130.3 %all-to-all-done.1 = bf16[64,14,2048]{2,1,0:T(8,128)(2,1)} async-done(((bf16[64,14,2048]{2,1,0:T(8,128)(2,1)}), bf16[64,14,2048]{2,1,0:T(8,128)(2,1)}, u32[]{:S(2)}, u32[]{:S(2)}) %all-to-all-start.1) | async-done | bytes 3670048 | tf_op jit(solution)/shard_map/all_to_all | solution.py:65
  201.6 5.8 %reshape.70 = bf16[896,2048]{1,0:T(8,128)(2,1)} reshape(bf16[64,14,2048]{2,1,0:T(8,128)(2,1)} %all-to-all-done.1) | data formatting | bytes 7340032 | tf_op jit(solution)/shard_map/reshape | solution.py:68
  207.5 0.0 copy-done
  207.5 0.0 copy-done.2
  207.5 0.0 copy-done.3
  207.5 3.3 multiply_reduce_fusion.1
  210.8 12.4 %psum.7 = f32[896]{0:T(1024)S(1)} all-reduce(f32[896]{0:T(1024)S(1)} %get-tuple-element.13), channel_id=1, replica_groups=mesh['dp'=64,'tower'=8] {'tower'}, use_global_device_ids=true, to_apply=%region_5.6 | all-reduce | flops 896 | bytes 7168 | tf_op jit(solution)/shard_map/psum | solution.py:32
  223.2 0.6 fusion.11
  223.8 3.1 convolution_convert_fusion
  226.9 6.0 %reshape.73 = bf16[64,14,2048]{2,1,0:T(8,128)(2,1)} reshape(bf16[896,2048]{1,0:T(8,128)(2,1)} %convolution_convert_fusion) | data formatting | bytes 7340032 | tf_op jit(solution)/shard_map/reshape | solution.py:82
  232.9 13.2 %all-to-all-start.3 = ((bf16[64,14,2048]{2,1,0:T(8,128)(2,1)}), bf16[64,14,2048]{2,1,0:T(8,128)(2,1)}, u32[]{:S(2)}, u32[]{:S(2)}) async-start(bf16[64,14,2048]{2,1,0:T(8,128)(2,1)} %reshape.73), calls=%async_computation.3 | async-start | bytes 8388608 | tf_op jit(solution)/shard_map/all_to_all | solution.py:81
  246.1 0.2 reduce-scatter.2.cloned.1.call-start
  246.4 119.7 %all-to-all-done.3 = bf16[64,14,2048]{2,1,0:T(8,128)(2,1)} async-done(((bf16[64,14,2048]{2,1,0:T(8,128)(2,1)}), bf16[64,14,2048]{2,1,0:T(8,128)(2,1)}, u32[]{:S(2)}, u32[]{:S(2)}) %all-to-all-start.3) | async-done | bytes 3670048 | tf_op jit(solution)/shard_map/all_to_all | solution.py:81
  366.1 6.0 %reshape.74 = bf16[896,2048]{1,0:T(8,128)(2,1)} reshape(bf16[64,14,2048]{2,1,0:T(8,128)(2,1)} %all-to-all-done.3) | data formatting | bytes 7340032 | tf_op jit(solution)/shard_map/reshape | solution.py:92
  372.1 5.9 %gather_fusion.2 = bf16[256,2048]{1,0:T(8,128)(2,1)} fusion(bf16[896,2048]{1,0:T(8,128)(2,1)} %reshape.74, s32[1024]{0:T(1024)S(1)} %pad_clamp_fusion), kind=kCustom, calls=%fused_computation.2 | custom fusion | bytes 2098176 | tf_op jit(solution)/shard_map/gather | solution.py:92
  377.9 0.0 reduce-scatter.2.cloned.1.call-update
  377.9 0.8 all_to_all.24
  378.7 17.6 %all-to-all-start.4 = ((bf16[64,1,14]{2,1,0:T(2,128)(2,1)}), bf16[64,1,14]{2,1,0:T(2,128)(2,1)S(1)}, u32[]{:S(2)}, u32[]{:S(2)}) async-start(bf16[64,1,14]{2,1,0:T(2,128)(2,1)} %all_to_all.24), calls=%async_computation.5 | async-start | bytes 65536 | tf_op jit(solution)/shard_map/all_to_all | solution.py:88
  396.3 4.9 %convolution_bitcast_fusion = f32[1,2048,256]{2,1,0:T(8,128)} fusion(bf16[896,2048]{1,0:T(8,128)(2,1)} %reshape.70, f32[896,256]{1,0:T(8,128)S(1)} %get-tuple-element.14, f32[896]{0:T(1024)S(1)} %get-tuple-element.11, f32[256]{0:T(256)S(1)} %bitcast.46), kind=kOutput, calls=%fused_computation.6 | convolution fusion | flops 941817856 | bytes 6689280 | tf_op jit(solution)/shard_map/dot_general | solution.py:36
  401.2 1.1 multiply_reduce_fusion
  402.3 5.0 %all-to-all-done.4 = bf16[64,1,14]{2,1,0:T(2,128)(2,1)S(1)} async-done(((bf16[64,1,14]{2,1,0:T(2,128)(2,1)}), bf16[64,1,14]{2,1,0:T(2,128)(2,1)S(1)}, u32[]{:S(2)}, u32[]{:S(2)}) %all-to-all-start.4) | async-done | bytes 1824 | tf_op jit(solution)/shard_map/all_to_all | solution.py:88
  407.3 0.1 reduce.3
  407.4 0.1 reshape.75
  407.6 2.4 gather_fusion.3
  410.0 16.7 %reduce-scatter.2.cloned.1.call-done = bf16[256,256]{1,0:T(8,128)(2,1)} async-done(((bf16[256,2048]{1,0:T(8,128)(2,1)}), bf16[256,256]{1,0:T(8,128)(2,1)}) %reduce-scatter.2.cloned.1.call-update) | async-done | bytes 131088 | tf_op jit(solution)/shard_map/reduce_scatter | solution.py:93
  (10 shorter events, 0.1 us)
Async XLA Ops:
  7.2 200.3 %copy-start = (bf16[1,2048,256]{2,1,0:T(8,128)(2,1)S(1)}, bf16[1,2048,256]{2,1,0:T(8,128)(2,1)}, u32[]{:S(2)}) copy-start(bf16[1,2048,256]{2,1,0:T(8,128)(2,1)} %param.12) | copy-start | bytes 3145732
  7.2 9.4 %copy-start.1 = (s32[256]{0:T(256)S(1)}, s32[256]{0:T(256)}, u32[]{:S(2)}) copy-start(s32[256]{0:T(256)} %param.9) | copy-start | bytes 3076
  9.2 20.3 %all-to-all-start = ((bf16[8,256,256]{2,1,0:T(8,128)(2,1)}), bf16[8,256,256]{2,1,0:T(8,128)(2,1)S(1)}, u32[]{:S(2)}, u32[]{:S(2)}) async-start(bf16[8,256,256]{2,1,0:T(8,128)(2,1)} %stack.8), calls=%async_computation | async-start | bytes 2097152 | tf_op jit(solution)/shard_map/all_to_all | solution.py:59
  29.5 27.8 %all-to-all-start.2 = ((bf16[64,14,2]{1,2,0:T(2,128)(2,1)}), bf16[64,14,2]{1,2,0:T(2,128)(2,1)S(1)}, u32[]{:S(2)}, u32[]{:S(2)}) async-start(bf16[64,14,2]{1,2,0:T(2,128)(2,1)} %copy.29), calls=%async_computation.2 | async-start | bytes 65536 | tf_op jit(solution)/shard_map/all_to_all | solution.py:66
  57.3 144.3 %all-to-all-start.1 = ((bf16[64,14,2048]{2,1,0:T(8,128)(2,1)}), bf16[64,14,2048]{2,1,0:T(8,128)(2,1)}, u32[]{:S(2)}, u32[]{:S(2)}) async-start(bf16[64,14,2048]{2,1,0:T(8,128)(2,1)} %reshape.69), calls=%async_computation.1 | async-start | bytes 8388608 | tf_op jit(solution)/shard_map/all_to_all | solution.py:65
  71.3 136.2 %copy-start.2 = (f32[1,256]{1,0:T(1,128)S(1)}, f32[1,256]{1,0:T(1,128)}, u32[]{:S(2)}) copy-start(f32[1,256]{1,0:T(1,128)} %param.14) | copy-start | bytes 3076
  71.3 136.2 %copy-start.3 = (f32[1,256]{1,0:T(1,128)S(1)}, f32[1,256]{1,0:T(1,128)}, u32[]{:S(2)}) copy-start(f32[1,256]{1,0:T(1,128)} %param.13) | copy-start | bytes 3076
  232.9 133.2 %all-to-all-start.3 = ((bf16[64,14,2048]{2,1,0:T(8,128)(2,1)}), bf16[64,14,2048]{2,1,0:T(8,128)(2,1)}, u32[]{:S(2)}, u32[]{:S(2)}) async-start(bf16[64,14,2048]{2,1,0:T(8,128)(2,1)} %reshape.73), calls=%async_computation.3 | async-start | bytes 8388608 | tf_op jit(solution)/shard_map/all_to_all | solution.py:81
  246.1 180.6 %reduce-scatter.2.cloned.1.call-start = ((), (), s32[]{:S(2)}) async-start(), calls=%async_computation.6 | async-start | bytes 1179648 | tf_op jit(solution)/shard_map/reduce_scatter | solution.py:93
  378.7 28.6 %all-to-all-start.4 = ((bf16[64,1,14]{2,1,0:T(2,128)(2,1)}), bf16[64,1,14]{2,1,0:T(2,128)(2,1)S(1)}, u32[]{:S(2)}, u32[]{:S(2)}) async-start(bf16[64,1,14]{2,1,0:T(2,128)(2,1)} %all_to_all.24), calls=%async_computation.5 | async-start | bytes 65536 | tf_op jit(solution)/shard_map/all_to_all | solution.py:88
Sparse Core Ops, SparseCore 0:
  378.1 48.6 reduce-scatter.1
